TPU v7x, 256 devices: a whole 4x4x8 slice. The times are simulated.
256 devices in a mesh: node: 16 (over x, y_lo, core), tm: 16 (over y_hi, z).
Axes of the slice: x: 4, y: 4 (y_hi: 2, y_lo: 2; y = y_hi * 2 + y_lo), z: 8, core: 2. Of those that a mesh axis runs over, the one named last changes fastest.
Arguments:
- series: bfloat16 [48, 4096, 256], P(None, ('node', 'tm')), may hold values from -16 to 16
- t_query: bfloat16 [256, 256], replicated, may hold values from -1 to 1
- t_key: bfloat16 [256, 256], replicated, may hold values from -5 to 5
- t_value: bfloat16 [256, 256], replicated, may hold values from -0.375 to 0.375
- t_out: bfloat16 [256, 256], replicated, may hold values from -0.375 to 0.375
- s_query: bfloat16 [256, 256], replicated, may hold values from -1 to 1
- s_key: bfloat16 [256, 256], replicated, may hold values from -5 to 5
- s_value: bfloat16 [256, 256], replicated, may hold values from -0.375 to 0.375
- s_out: bfloat16 [256, 256], replicated, may hold values from -0.375 to 0.375
- gain_first: float32 [256], replicated, may hold values from 0.25 to 1.75
- gain_second: float32 [256], replicated, may hold values from 0.25 to 1.75
Outputs:
- output: bfloat16 [48, 4096, 256], P(None, ('node', 'tm'))
All inputs are finite; a program needn't handle non-finite values.
Results may differ from a plain program's by a relative error of at most 0.0092.
Values may be sent and summed in bfloat16 or wider, within the bound.
A program may use at most 64 MiB of HBM per device.

v0:
```python
import math

import jax
import jax.numpy as jnp
from jax import lax
from jax.sharding import PartitionSpec as P

HEADS = 8


epsilon = 1e-05
neg_large = -1e30
key_block = 128


def layer_norm(values, gain):
    center = values - jnp.mean(values, axis=-1, keepdims=True)
    spread = jnp.mean(center * center, axis=-1, keepdims=True)
    return center * lax.rsqrt(spread + epsilon) * gain


def linear(values, weight):
    flattened = values.reshape(-1, values.shape[-1])
    result = jnp.dot(flattened, weight, preferred_element_type=jnp.float32)
    return result.reshape(values.shape[:-1] + (weight.shape[1],))


def temporal_part(series, t_query, t_key, t_value, t_out):
    step_count, node_count, model_width = series.shape
    head_dim = model_width // HEADS
    shaped = (step_count, node_count, HEADS, head_dim)
    queries = linear(series, t_query).astype(jnp.bfloat16).reshape(shaped)
    key_rows = linear(series, t_key).astype(jnp.bfloat16).reshape(shaped)
    value_rows = linear(series, t_value).astype(jnp.bfloat16).reshape(shaped)
    scores = jnp.einsum(
        "snhe,tnhe->nhst", queries, key_rows, preferred_element_type=jnp.float32
    ) * (1.0 / math.sqrt(head_dim))
    causal = lax.broadcasted_iota(jnp.int32, (step_count, step_count), 0) >= lax.broadcasted_iota(
        jnp.int32, (step_count, step_count), 1
    )
    scores = jnp.where(causal, scores, -jnp.inf)
    row_max = jnp.max(scores, axis=-1, keepdims=True)
    weights_exp = jnp.exp(scores - row_max)
    total = jnp.sum(weights_exp, axis=-1)
    mixed_heads = jnp.einsum(
        "nhst,tnhe->snhe",
        weights_exp.astype(jnp.bfloat16),
        value_rows,
        preferred_element_type=jnp.float32,
    )
    mixed_heads = mixed_heads / jnp.transpose(total, (2, 0, 1))[..., None]
    mixed_heads = mixed_heads.astype(jnp.bfloat16).reshape(step_count, node_count, model_width)
    return series.astype(jnp.float32) + linear(mixed_heads, t_out)


def attend_block(state, queries, key_rows, value_rows, scale):
    row_max, total, accum = state
    step_count, row_count, model_width = key_rows.shape
    head_dim = model_width // HEADS
    keys_split = key_rows.reshape(step_count, row_count, HEADS, head_dim)
    values_split = value_rows.reshape(step_count, row_count, HEADS, head_dim)
    scores = (
        jnp.einsum("tqhe,tkhe->thqk", queries, keys_split, preferred_element_type=jnp.float32)
        * scale
    )
    new_max = jnp.maximum(row_max, jnp.max(scores, axis=-1))
    rescale = jnp.exp(row_max - new_max)
    weights_exp = jnp.exp(scores - new_max[..., None])
    total = total * rescale + jnp.sum(weights_exp, axis=-1)
    update = jnp.einsum(
        "thqk,tkhe->tqhe",
        weights_exp.astype(jnp.bfloat16),
        values_split,
        preferred_element_type=jnp.float32,
    )
    accum = accum * jnp.transpose(rescale, (0, 2, 1))[..., None] + update
    return (new_max, total, accum)


def attend_rows(state, queries, key_rows, value_rows, scale):
    row_count = key_rows.shape[1]
    blocks = row_count // key_block

    def split_rows(rows):
        reshaped = rows.reshape(rows.shape[0], blocks, key_block, rows.shape[2])
        return jnp.moveaxis(reshaped, 1, 0)

    def visit(inner, pair):
        return (attend_block(inner, queries, pair[0], pair[1], scale), None)

    state, unused = lax.scan(visit, state, (split_rows(key_rows), split_rows(value_rows)))
    return state


def shards(
    series, t_query, t_key, t_value, t_out, s_query, s_key, s_value, s_out, gain_first, gain_second
):
    first = temporal_part(series, t_query, t_key, t_value, t_out)
    hidden_nodes = layer_norm(first, gain_first).astype(jnp.bfloat16)
    hidden_steps = lax.all_to_all(hidden_nodes, "tm", split_axis=0, concat_axis=1, tiled=True)
    step_count, node_count, model_width = hidden_steps.shape
    head_dim = model_width // HEADS
    scale = 1.0 / math.sqrt(head_dim)
    queries = (
        linear(hidden_steps, s_query)
        .astype(jnp.bfloat16)
        .reshape(step_count, node_count, HEADS, head_dim)
    )
    initial = (
        jnp.full((step_count, HEADS, node_count), neg_large, jnp.float32),
        jnp.zeros((step_count, HEADS, node_count), jnp.float32),
        jnp.zeros((step_count, node_count, HEADS, head_dim), jnp.float32),
    )
    key_rows = linear(hidden_steps, s_key).astype(jnp.bfloat16)
    value_rows = linear(hidden_steps, s_value).astype(jnp.bfloat16)
    final = attend_rows(
        initial,
        queries,
        lax.all_gather(key_rows, "node", axis=1, tiled=True),
        lax.all_gather(value_rows, "node", axis=1, tiled=True),
        scale,
    )
    row_max, total, accum = final
    spatial = accum / jnp.transpose(total, (0, 2, 1))[..., None]
    spatial = spatial.astype(jnp.bfloat16).reshape(step_count, node_count, model_width)
    returned = lax.all_to_all(spatial, "tm", split_axis=1, concat_axis=0, tiled=True)
    second = hidden_nodes.astype(jnp.float32) + linear(returned, s_out)
    return layer_norm(second, gain_second).astype(jnp.bfloat16)


def solution(mesh):
    in_specs = (P(None, ("node", "tm"), None), P(), P(), P(), P(), P(), P(), P(), P(), P(), P())
    out_specs = P(None, ("node", "tm"), None)
    return jax.shard_map(shards, mesh=mesh, in_specs=in_specs, out_specs=out_specs, check_vma=False)
```

profile of v0, /device:TPU:1, one launch (start us, length us, event | category | flops | bytes accessed | tf_op | source)
XLA Modules:
  0.0 373.1 jit_solution(11192615520407402007)
XLA Ops:
  16.7 23.8 %all_to_all.30 = bf16[48,16,256]{2,1,0:T(8,128)(2,1)S(1)} all-to-all(bf16[48,16,256]{2,1,0:T(8,128)(2,1)S(1)} %multiply_convert_fusion.1), channel_id=1, replica_groups=mesh['node'=16,'tm'=16] {'tm'}, dimensions={0} | all-to-all | bytes 786432 | tf_op jit(solution)/shard_map/all_to_all | solution.py:100
  43.7 42.0 %all-gather.3.cloned.1.call-done = bf16[3,4096,256]{2,1,0:T(8,128)(2,1)} async-done(((bf16[3,256,256]{2,1,0:T(8,128)(2,1)}), bf16[3,4096,256]{2,1,0:T(8,128)(2,1)}) %all-gather.3.cloned.1.call-update) | async-done | bytes 6291472 | tf_op jit(solution)/shard_map/all_gather | solution.py:119
  85.7 8.7 %copy.53 = bf16[3,32,128,256]{2,3,0,1:T(8,128)(2,1)} copy(bf16[3,32,128,256]{3,2,1,0:T(8,128)(2,1)} %bitcast.116) | data formatting | bytes 12582912 | tf_op jit(solution)/shard_map/reshape | solution.py:85
  94.4 38.9 %all-gather.5.cloned.1.call-done = bf16[3,4096,256]{2,1,0:T(8,128)(2,1)} async-done(((bf16[3,256,256]{2,1,0:T(8,128)(2,1)}), bf16[3,4096,256]{2,1,0:T(8,128)(2,1)}) %all-gather.5.cloned.1.call-update) | async-done | bytes 6291472 | tf_op jit(solution)/shard_map/all_gather | solution.py:120
  133.3 8.6 %copy.55 = bf16[3,32,128,256]{2,3,0,1:T(8,128)(2,1)} copy(bf16[3,32,128,256]{3,2,1,0:T(8,128)(2,1)} %bitcast.117) | data formatting | bytes 12582912 | tf_op jit(solution)/shard_map/reshape | solution.py:85
  141.9 196.8 %while.15 = (s32[]{:T(128)}, f32[3,8,256]{2,1,0:T(8,128)S(1)}, f32[3,8,256]{2,1,0:T(8,128)S(1)}, f32[3,256,8,32]{1,3,2,0:T(8,128)}, bf16[32,3,128,256]{2,3,1,0:T...) while((s32[]{:T(128)}, f32[3,8,256]{2,1,0:T(8,128)S(1)}, ...), condition=%wide.region_7.8_spmd.clone, body=%wide.region_4.7_spmd.clone.sunk | while | flops 107581440 | bytes 12976237 | solution.py:91
  149.7 2.8 fusion.66
  155.9 2.8 fusion.66
  162.0 2.8 fusion.66
  168.2 2.8 fusion.66
  174.4 2.8 fusion.66
  180.6 2.8 fusion.66
  186.8 2.8 fusion.66
  193.0 2.8 fusion.66
  199.2 2.8 fusion.66
  205.3 2.8 fusion.66
  211.5 2.8 fusion.66
  217.7 2.8 fusion.66
  223.9 2.8 fusion.66
  230.1 2.8 fusion.66
  236.3 2.8 fusion.66
  242.5 2.8 fusion.66
  248.7 2.8 fusion.66
  254.8 2.8 fusion.66
  261.0 2.8 fusion.66
  267.2 2.8 fusion.66
  273.4 2.8 fusion.66
  279.6 2.8 fusion.66
  298.1 2.8 fusion.66
  316.7 2.8 fusion.66
  335.3 2.8 fusion.66
  340.3 24.1 %all_to_all.31 = bf16[3,256,256]{2,0,1:T(4,128)(2,1)S(1)} all-to-all(bf16[3,256,256]{2,0,1:T(4,128)(2,1)S(1)} %copy.56), channel_id=1, replica_groups=mesh['node'=16,'tm'=16] {'tm'}, dimensions={1} | all-to-all | bytes 786432 | tf_op jit(solution)/shard_map/all_to_all | solution.py:126
  (259 shorter events, 141.6 us)
Async XLA Ops:
  6.5 9.1 %copy-start = (bf16[256,256]{1,0:T(8,128)(2,1)S(1)}, bf16[256,256]{1,0:T(8,128)(2,1)}, u32[]{:S(2)}) copy-start(bf16[256,256]{1,0:T(8,128)(2,1)} %param.17) | copy-start | bytes 393220
  6.5 3.8 %copy-start.1 = (bf16[48,16,256]{2,1,0:T(8,128)(2,1)S(1)}, bf16[48,16,256]{2,1,0:T(8,128)(2,1)}, u32[]{:S(2)}) copy-start(bf16[48,16,256]{2,1,0:T(8,128)(2,1)} %param.13) | copy-start | bytes 1179652
  6.5 3.8 %copy-start.5 = (bf16[256,256]{1,0:T(8,128)(2,1)S(1)}, bf16[256,256]{1,0:T(8,128)(2,1)}, u32[]{:S(2)}) copy-start(bf16[256,256]{1,0:T(8,128)(2,1)} %param.16) | copy-start | bytes 393220
  6.5 79.2 %all-gather.3.cloned.1.call-start = ((), (), s32[]{:S(2)}) async-start(), calls=%async_computation.2 | async-start | bytes 6684672 | tf_op jit(solution)/shard_map/all_gather | solution.py:119
  12.1 2.0 copy-start.4
  14.9 1.4 copy-start.10
  15.0 25.5 %copy-start.6 = (bf16[256,256]{1,0:T(8,128)(2,1)S(1)}, bf16[256,256]{1,0:T(8,128)(2,1)}, u32[]{:S(2)}) copy-start(bf16[256,256]{1,0:T(8,128)(2,1)} %param.19) | copy-start | bytes 393220
  15.7 25.9 %copy-start.7 = (bf16[256,256]{1,0:T(8,128)(2,1)S(1)}, bf16[256,256]{1,0:T(8,128)(2,1)}, u32[]{:S(2)}) copy-start(bf16[256,256]{1,0:T(8,128)(2,1)} %param.20) | copy-start | bytes 393220
  16.0 26.6 %copy-start.8 = (bf16[256,256]{1,0:T(8,128)(2,1)S(1)}, bf16[256,256]{1,0:T(8,128)(2,1)}, u32[]{:S(2)}) copy-start(bf16[256,256]{1,0:T(8,128)(2,1)} %param.18) | copy-start | bytes 393220
  16.7 23.8 %copy-start.2 = (bf16[48,16,256]{2,1,0:T(8,128)(2,1)}, bf16[48,16,256]{2,1,0:T(8,128)(2,1)S(1)}, u32[]{:S(2)}) copy-start(bf16[48,16,256]{2,1,0:T(8,128)(2,1)S(1)} %multiply_convert_fusion.1) | copy-start | bytes 1179652
  41.5 91.7 %all-gather.5.cloned.1.call-start = ((), (), s32[]{:S(2)}) async-start(), calls=%async_computation.3 | async-start | bytes 6684672 | tf_op jit(solution)/shard_map/all_gather | solution.py:120
  338.7 25.8 %copy-start.3 = (bf16[48,16,256]{2,1,0:T(8,128)(2,1)S(1)}, bf16[48,16,256]{2,1,0:T(8,128)(2,1)}, u32[]{:S(2)}) copy-start(bf16[48,16,256]{2,1,0:T(8,128)(2,1)} %copy-done.2) | copy-start | bytes 1179652
  338.7 25.8 %copy-start.9 = (bf16[256,256]{1,0:T(8,128)(2,1)S(1)}, bf16[256,256]{1,0:T(8,128)(2,1)}, u32[]{:S(2)}) copy-start(bf16[256,256]{1,0:T(8,128)(2,1)} %param.21) | copy-start | bytes 393220
  340.0 25.2 %copy-start.11 = (f32[256]{0:T(256)S(1)}, f32[256]{0:T(256)}, u32[]{:S(2)}) copy-start(f32[256]{0:T(256)} %param.23) | copy-start | bytes 3076
Sparse Core Ops, SparseCore 0:
  41.6 44.0 all-gather.2
  87.5 45.7 all-gather.4
where the time goes:
time: 378 us; the launch traced here: 373 us
  matrix products  149 us (39%)
  waiting for transfers between devices  80.9 us (21%)
  local copies, waits for them, and re-layouts  54.8 us (14%)
  blocking collectives  47.9 us (13%)
  other arithmetic  24.8 us (7%)
  between operations  13.7 us (4%)
    dot_general x32, matrix products, attend_block(): jnp.einsum('thqk,tkhe->tqhe', weights_exp.astype(jnp.bfloat16), values_sp...  88.6 us
    dot_general x32, matrix products, attend_block(): jnp.einsum('tqhe,tkhe->thqk', queries, keys_split, preferred_element_type...  52.2 us
    all_gather x1, waiting for transfers between devices, shards(): lax.all_gather(key_rows, 'node', axis=1, tiled=True)  42 us
    all_gather x1, waiting for transfers between devices, shards(): lax.all_gather(value_rows, 'node', axis=1, tiled=True)  38.9 us
    dynamic_slice x32, local copies, waits for them, and re-layouts, attend_rows(): lax.scan(visit, state, (split_rows(key_rows), split_rows(value_rows)))  33.7 us
    all_to_all x1, blocking collectives, shards(): lax.all_to_all(spatial, 'tm', split_axis=1, concat_axis=0, tiled=True)  24.1 us
    all_to_all x1, blocking collectives, shards(): lax.all_to_all(hidden_nodes, 'tm', split_axis=0, concat_axis=1, tiled=True)  23.8 us
    reduce_sum x32, other arithmetic, attend_block(): total = total * rescale + jnp.sum(weights_exp, axis=-1)  19.6 us
  transfers between devices with their start and end apart: 2, of which 2 were waited for; matrix products, arithmetic and copies ran while one was open for 3% of the time, Pallas kernels for 0%

commit v1 on v0

v1 whole, which is shorter than its diff:
```python
import functools
import math

import jax
import jax.numpy as jnp
from jax import lax
from jax.experimental import pallas as pl
from jax.experimental.pallas import tpu as pltpu
from jax.sharding import PartitionSpec as P

HEADS = 8
epsilon = 1e-05
f32, bf16 = jnp.float32, jnp.bfloat16
MESH = pl.DeviceIdType.MESH


def layer_norm(values, gain):
    center = values - jnp.mean(values, axis=-1, keepdims=True)
    spread = jnp.mean(center * center, axis=-1, keepdims=True)
    return center * lax.rsqrt(spread + epsilon) * gain


def linear(values, weight):
    flattened = values.reshape(-1, values.shape[-1])
    result = jnp.dot(flattened, weight, preferred_element_type=f32)
    return result.reshape(values.shape[:-1] + (weight.shape[1],))


def temporal_part(series, t_query, t_key, t_value, t_out):
    step_count, node_count, model_width = series.shape
    head_dim = model_width // HEADS
    shaped = (step_count, node_count, HEADS, head_dim)
    queries = linear(series, t_query).astype(bf16).reshape(shaped)
    key_rows = linear(series, t_key).astype(bf16).reshape(shaped)
    value_rows = linear(series, t_value).astype(bf16).reshape(shaped)
    scores = jnp.einsum(
        "snhe,tnhe->nhst", queries, key_rows, preferred_element_type=f32
    ) * (1.0 / math.sqrt(head_dim))
    causal = lax.broadcasted_iota(jnp.int32, (step_count, step_count), 0) >= lax.broadcasted_iota(
        jnp.int32, (step_count, step_count), 1
    )
    scores = jnp.where(causal, scores, -jnp.inf)
    row_max = jnp.max(scores, axis=-1, keepdims=True)
    weights_exp = jnp.exp(scores - row_max)
    total = jnp.sum(weights_exp, axis=-1)
    mixed_heads = jnp.einsum(
        "nhst,tnhe->snhe", weights_exp.astype(bf16), value_rows, preferred_element_type=f32
    )
    mixed_heads = mixed_heads / jnp.transpose(total, (2, 0, 1))[..., None]
    mixed_heads = mixed_heads.astype(bf16).reshape(step_count, node_count, model_width)
    return series.astype(f32) + linear(mixed_heads, t_out)


def dot_t(a, b):
    return lax.dot_general(a, b, (((1,), (1,)), ((), ())), preferred_element_type=f32)


def dot(a, b):
    return jnp.dot(a, b, preferred_element_type=f32)


def spatial_kernel(
    hid, wq, wk, wv, wo, gain, out,
    keys_in, k_buf, v_buf, q_mask, acc, row_max, result,
    a_send, a_recv, n_send, n_recv, s_send, s_recv, r_send, r_recv,
):
    steps, rows, width = keys_in.shape
    node = lax.axis_index("node")
    me = lax.axis_index("tm")
    groups = 16
    block = rows // 16
    slab = block // groups
    core = node % 2
    y_lo = (node // 2) % 2
    x = node // 4
    sibling = node + 1 - 2 * core
    y_peer = node + 2 - 4 * y_lo
    right = ((x + 1) % 4) * 4 + node % 4
    left = ((x + 3) % 4) * 4 + node % 4
    head_dim = width // HEADS

    barrier = pltpu.get_barrier_semaphore()
    for other in (sibling, y_peer, right, left):
        pl.semaphore_signal(barrier, inc=1, device_id={"node": other}, device_id_type=MESH)

    def greet(k, carry):
        pl.semaphore_signal(
            barrier, inc=1, device_id={"tm": (me + k) % groups}, device_id_type=MESH
        )
        return carry

    lax.fori_loop(1, groups, greet, 0)
    pl.semaphore_wait(barrier, groups - 1 + 4)

    def scatter_copy(t, j):
        return pltpu.make_async_remote_copy(
            src_ref=hid.at[steps * j + t],
            dst_ref=keys_in.at[t, pl.ds(pl.multiple_of(me * slab, slab), slab), :],
            send_sem=a_send.at[t],
            recv_sem=a_recv.at[t],
            device_id={"tm": j},
            device_id_type=MESH,
        )

    for t in range(steps):
        def scatter(k, carry):
            scatter_copy(t, (me + k) % groups).start()
            return carry

        lax.fori_loop(1, groups, scatter, 0)
    for t in range(steps):
        keys_in[t, pl.ds(pl.multiple_of(me * slab, slab), slab), :] = hid[steps * me + t]

    def wait_bytes(ref, sem):
        pltpu.make_async_copy(ref, ref, sem).wait()

    def send(t, src, dst, count, index, other):
        return pltpu.make_async_remote_copy(
            src_ref=keys_in.at[t, pl.ds(src * block, count * block), :],
            dst_ref=keys_in.at[t, pl.ds(dst * block, count * block), :],
            send_sem=n_send.at[t, index],
            recv_sem=n_recv.at[t, index],
            device_id={"node": other},
            device_id_type=MESH,
        )

    def to_sibling(t, src, count, index):
        return pltpu.make_async_remote_copy(
            src_ref=keys_in.at[t, pl.ds(src * block, count * block), :],
            dst_ref=keys_in.at[t, pl.ds((src + 2) * block, count * block), :],
            send_sem=s_send.at[t, index],
            recv_sem=s_recv.at[t, index],
            device_id={"node": sibling},
            device_id_type=MESH,
        )

    def copies(t):
        return [
            send(t, 0, 1, 1, 0, y_peer),
            send(t, 0, 4, 1, 1, right),
            send(t, 0, 8, 1, 2, left),
            send(t, 1, 5, 1, 3, right),
            send(t, 1, 9, 1, 4, left),
            send(t, 4, 12, 1, 5, right),
            send(t, 9, 13, 1, 6, left),
        ]

    def sib_copies(t):
        return [
            to_sibling(t, 0, 1, 0),
            to_sibling(t, 1, 1, 1),
            to_sibling(t, 4, 2, 2),
            to_sibling(t, 8, 2, 3),
            to_sibling(t, 12, 2, 4),
        ]

    def own_ready(t):
        wait_bytes(keys_in.at[t, pl.ds(0, block - slab), :], a_recv.at[t])
        c, s = copies(t), sib_copies(t)
        c[0].start()
        s[0].start()
        c[1].start()
        c[2].start()

    def y_ready(t):
        c, s = copies(t), sib_copies(t)
        c[0].wait_recv()
        s[1].start()
        c[3].start()
        c[4].start()

    def sides_ready(t):
        c, s = copies(t), sib_copies(t)
        c[1].wait_recv()
        c[3].wait_recv()
        c[2].wait_recv()
        c[4].wait_recv()
        c[5].start()
        c[6].start()
        s[2].start()
        s[3].start()

    def opposite_ready(t):
        c, s = copies(t), sib_copies(t)
        c[5].wait_recv()
        c[6].wait_recv()
        s[4].start()

    own_ready(0)
    chunk = 4 * block
    v_buf[:, :, width // 2:] = jnp.ones((2, chunk, width // 2), bf16)
    scale = math.log2(math.e) / math.sqrt(head_dim)
    y_ready(0)

    def tick(g, carry):
        t = g // 8
        u = g % 8
        part = u // 2
        half = u % 2

        @pl.when(u == 0)
        def _():
            own = keys_in[t, pl.ds(0, block), :]
            q = (dot(own, wq[...]) * scale).astype(bf16)
            lane = lax.broadcasted_iota(jnp.int32, (block, width), 1) // head_dim
            for h in range(HEADS):
                q_mask[h] = jnp.where(lane == h, q, jnp.zeros_like(q))
            acc[...] = jnp.zeros_like(acc)
            row_max[...] = jnp.full_like(row_max, -1e30)
            s = sib_copies(t)
            s[0].wait_recv()
            s[1].wait_recv()

        @pl.when(u == 1)
        def _():
            sides_ready(t)

        @pl.when(u == 2)
        def _():
            sib_copies(t)[2].wait_recv()

        @pl.when((u == 3) & (t < steps - 1))
        def _():
            own_ready(t + 1)

        @pl.when(u == 4)
        def _():
            sib_copies(t)[3].wait_recv()

        @pl.when(u == 5)
        def _():
            opposite_ready(t)

        @pl.when((u == 5) & (t < steps - 1))
        def _():
            y_ready(t + 1)

        @pl.when(u == 6)
        def _():
            sib_copies(t)[4].wait_recv()

        @pl.when(half == 0)
        def _():
            rows_in = keys_in[t, pl.ds(pl.multiple_of(part * chunk, chunk), chunk), :]
            k_buf[...] = dot(rows_in, wk[...]).astype(bf16)
            v = dot(rows_in, wv[...]).astype(bf16)
            v_buf[0, :, : width // 2] = v[:, : width // 2]
            v_buf[1, :, : width // 2] = v[:, width // 2 :]

        for i in range(HEADS // 2):
            h = half * (HEADS // 2) + i
            s = dot_t(q_mask[h], k_buf[...])
            old = row_max[h]
            new = jnp.maximum(old, jnp.max(s, axis=1, keepdims=True))
            p = jnp.exp2(s - new[:, 0:1]).astype(bf16)
            fade = jnp.exp2(old - new)
            acc[h] = acc[h] * fade[:, 0:1] + dot(p, v_buf[half])
            row_max[h] = new

        @pl.when(u == 7)
        def _():
            lane = lax.broadcasted_iota(jnp.int32, (block, width // 2), 1) // head_dim
            sides = []
            for s in range(2):
                mixed = jnp.zeros((block, width // 2), f32)
                for i in range(HEADS // 2):
                    a = acc[s * (HEADS // 2) + i]
                    mixed = jnp.where(lane == i, a[:, : width // 2] / a[:, width // 2 :], mixed)
                sides.append(mixed.astype(bf16))
            mixed = jnp.concatenate(sides, axis=1)
            own = keys_in[t, pl.ds(0, block), :].astype(f32)
            second = own + dot(mixed, wo[...])
            result[t] = layer_norm(second, gain[...]).astype(bf16)

            def give(k, carry):
                give_copy(t, (me + k) % groups).start()
                return carry

            lax.fori_loop(1, groups, give, 0)

        return carry

    def give_copy(t, j):
        return pltpu.make_async_remote_copy(
            src_ref=result.at[t, pl.ds(pl.multiple_of(j * slab, slab), slab), :],
            dst_ref=out.at[steps * me + t],
            send_sem=r_send.at[t],
            recv_sem=r_recv.at[t],
            device_id={"tm": j},
            device_id_type=MESH,
        )

    lax.fori_loop(0, 8 * steps, tick, 0)

    for t in range(steps):
        out[steps * me + t] = result[t, pl.ds(pl.multiple_of(me * slab, slab), slab), :]
    for t in range(steps):
        wait_bytes(keys_in.at[t, pl.ds(0, block - slab), :], a_send.at[t])
        for c in copies(t) + sib_copies(t):
            c.wait_send()
        wait_bytes(result.at[t, pl.ds(0, block - slab), :], r_send.at[t])
        wait_bytes(result.at[t, pl.ds(0, block - slab), :], r_recv.at[t])


def spatial(hidden, s_query, s_key, s_value, s_out, gain):
    total_steps, nodes, width = hidden.shape
    steps = total_steps // 16
    block = nodes * 16
    chunk = 4 * block
    vmem = pl.BlockSpec(memory_space=pltpu.VMEM)
    return pl.pallas_call(
        spatial_kernel,
        out_shape=jax.ShapeDtypeStruct(hidden.shape, bf16),
        in_specs=[vmem] * 6,
        out_specs=vmem,
        scratch_shapes=[
            pltpu.VMEM((steps, 16 * block, width), bf16),
            pltpu.VMEM((chunk, width), bf16),
            pltpu.VMEM((2, chunk, width), bf16),
            pltpu.VMEM((HEADS, block, width), bf16),
            pltpu.VMEM((HEADS, block, width), f32),
            pltpu.VMEM((HEADS, block, 128), f32),
            pltpu.VMEM((steps, block, width), bf16),
            pltpu.SemaphoreType.DMA((steps,)),
            pltpu.SemaphoreType.DMA((steps,)),
            pltpu.SemaphoreType.DMA((steps, 7)),
            pltpu.SemaphoreType.DMA((steps, 7)),
            pltpu.SemaphoreType.DMA((steps, 5)),
            pltpu.SemaphoreType.DMA((steps, 5)),
            pltpu.SemaphoreType.DMA((steps,)),
            pltpu.SemaphoreType.DMA((steps,)),
        ],
        compiler_params=pltpu.CompilerParams(
            collective_id=0, has_side_effects=True, vmem_limit_bytes=48 * 2**20
        ),
    )(hidden, s_query, s_key, s_value, s_out, gain.reshape(1, width))


def shards(
    series, t_query, t_key, t_value, t_out, s_query, s_key, s_value, s_out, gain_first, gain_second
):
    first = temporal_part(series, t_query, t_key, t_value, t_out)
    hidden = layer_norm(first, gain_first).astype(bf16)
    return spatial(hidden, s_query, s_key, s_value, s_out, gain_second)


def solution(mesh):
    in_specs = (P(None, ("node", "tm"), None), P(), P(), P(), P(), P(), P(), P(), P(), P(), P())
    out_specs = P(None, ("node", "tm"), None)
    return jax.shard_map(shards, mesh=mesh, in_specs=in_specs, out_specs=out_specs, check_vma=False)
```

time: 378 us -> 110 us (0.29); the launches traced: 373 us -> 109 us
  matrix products: 149 us -> 10.5 us
  Pallas kernels: 0 us -> 89 us
  waiting for transfers between devices: 80.9 us -> 0 us
  blocking collectives: 47.9 us -> 0 us
  local copies, waits for them, and re-layouts: 54.8 us -> 8.09 us
  other arithmetic: 24.8 us -> 1.63 us
  between operations: 13.7 us -> 0.18 us
    dot_general x74 -> x6, matrix products: 149 us -> 10.5 us  [the longest x4 4.93 us: linear(): result = jnp.dot(flattened, weight, preferred_element_type=f32)]
    pallas_call x0 -> x1, Pallas kernels: none -> 89 us  [spatial(): pl.pallas_call(spatial_kernel, out_shape=jax.ShapeDtypeStruct(hidden.shap...]
    all_gather x2 -> x0, waiting for transfers between devices: 80.9 us -> none  [the longest x1 42 us: shards(): lax.all_gather(key_rows, 'node', axis=1, tiled=True)]
    all_to_all x2 -> x0, blocking collectives: 47.9 us -> none  [the longest x1 24.1 us: shards(): lax.all_to_all(spatial, 'tm', split_axis=1, concat_axis=0, tiled=True)]
    dynamic_slice x32 -> x0, local copies, waits for them, and re-layouts: 33.7 us -> none  [attend_rows(): lax.scan(visit, state, (split_rows(key_rows), split_rows(value_rows)))]
    reduce_sum x32 -> x0, other arithmetic: 19.6 us -> none  [attend_block(): total = total * rescale + jnp.sum(weights_exp, axis=-1)]
    reshape x6 -> x3, local copies, waits for them, and re-layouts: 20.2 us -> 5.46 us  [the longest x1 2.47 us: temporal_part(): value_rows = linear(series, t_value).astype(bf16).reshape(shaped)]
  transfers between devices with their start and end apart: 2 -> 0, of which waited for: 2 -> 0; matrix products, arithmetic and copies ran while one was open for 3% -> 0% of each run, Pallas kernels for 0% -> 0%
where the time goes in v1:
time: 110 us; the launch traced here: 109 us
  Pallas kernels  89 us (81%)
  matrix products  10.5 us (10%)
  local copies, waits for them, and re-layouts  8.09 us (7%)
  other arithmetic  1.63 us (1%)
    pallas_call x1, Pallas kernels, spatial(): pl.pallas_call(spatial_kernel, out_shape=jax.ShapeDtypeStruct(hidden.shap...  89 us
    dot_general x4, matrix products, linear(): result = jnp.dot(flattened, weight, preferred_element_type=f32)  4.93 us
    dot_general x1, matrix products, temporal_part(): jnp.einsum('nhst,tnhe->snhe', weights_exp.astype(bf16), value_rows, prefe...  3.09 us
    dot_general x1, matrix products, temporal_part(): jnp.einsum('snhe,tnhe->nhst', queries, key_rows, preferred_element_type=f32)  2.48 us
    reshape x1, local copies, waits for them, and re-layouts, temporal_part(): value_rows = linear(series, t_value).astype(bf16).reshape(shaped)  2.47 us

profile of v1, /device:TPU:1, one launch (start us, length us, event | category | flops | bytes accessed | tf_op | source)
XLA Modules:
  0.0 109.4 jit_solution(14817005420048429722)
XLA Ops:
  0.0 0.0 copy-start
  0.0 1.3 %convolution_convert_fusion.1 = bf16[48,16,256]{2,1,0:T(8,128)(2,1)S(1)} fusion(bf16[48,16,256]{2,1,0:T(8,128)(2,1)} %param.11, bf16[256,256]{1,0:T(8,128)(2,1)} %param.12), kind=kOutput, calls=%fused_computation.13 | convolution fusion | flops 100859904 | bytes 917504 | tf_op jit(solution)/shard_map/dot_general | solution.py:25
  1.3 1.5 %copy.24 = bf16[48,16,256]{0,2,1:T(8,128)(2,1)} copy(bf16[48,16,256]{2,1,0:T(8,128)(2,1)S(1)} %convolution_convert_fusion.1) | data formatting | bytes 786432 | tf_op jit(solution)/shard_map/reshape | solution.py:33
  2.8 1.3 %convolution_convert_fusion = bf16[48,16,256]{2,1,0:T(8,128)(2,1)S(1)} fusion(bf16[48,16,256]{2,1,0:T(8,128)(2,1)} %param.11, bf16[256,256]{1,0:T(8,128)(2,1)} %param.13), kind=kOutput, calls=%fused_computation.12 | convolution fusion | flops 100859904 | bytes 917504 | tf_op jit(solution)/shard_map/dot_general | solution.py:25
  4.1 1.5 %copy.25 = bf16[48,16,256]{0,2,1:T(8,128)(2,1)} copy(bf16[48,16,256]{2,1,0:T(8,128)(2,1)S(1)} %convolution_convert_fusion) | data formatting | bytes 786432 | tf_op jit(solution)/shard_map/reshape | solution.py:34
  5.6 0.0 copy-start.7
  5.6 2.5 %fusion = (f32[16,8,48]{2,1,0:T(8,128)S(1)}, f32[16,8,48,48]{2,3,1,0:T(8,128)S(1)}) fusion(pred[48,48]{0,1:T(8,128)(4,1)S(1)} %iota_compare_fusion, bf16[48,16,8,32]{0,3,2,1:T(8,128)(2,1)} %bitcast.32, bf16[48,16,8,32]{0,3,2,1:T(8,128)(2,1)} %bitcast.33), kind=kOutput, calls=%fused_computation.2 | convolution fusion | flops 19752960 | bytes 1992960 | tf_op jit(solution)/shard_map/snhe,tnhe->nhst/dot_general | solution.py:36
  8.1 1.0 fusion.1
  9.1 0.0 copy-done.6
  9.2 0.0 copy-done.7
  9.2 1.0 convolution_convert_fusion.2
  10.2 2.5 %copy.23 = bf16[48,16,256]{0,2,1:T(8,128)(2,1)} copy(bf16[48,16,256]{2,1,0:T(8,128)(2,1)} %convolution_convert_fusion.2) | data formatting | bytes 786432 | tf_op jit(solution)/shard_map/reshape | solution.py:35
  12.6 3.1 %fusion.3 = bf16[48,16,8,32]{0,3,2,1:T(8,128)(2,1)} fusion(bf16[48,16,8,32]{0,3,2,1:T(8,128)(2,1)} %bitcast.34, f32[16,8,48,48]{2,3,1,0:T(8,128)S(1)} %get-tuple-element.6, f32[16,8,48]{2,1,0:T(8,128)S(1)} %get-tuple-element.5, pred[48,48]{0,1:T(8,128)(4,1)S(1)} %iota_compare_fusion, f32[48,16,8]{0,2,1:T(8,128)S(1)} %bitcast.36), kind=kOutput, calls=%fused_computation.6 | convolution fusion | flops 20447232 | bytes 2017536 | tf_op jit(solution)/shard_map/nhst,tnhe->snhe/dot_general | solution.py:46
  15.7 0.0 copy-start.8
  15.7 0.0 copy-start.1
  15.7 0.0 copy-start.2
  15.7 0.0 copy-start.3
  15.7 0.0 copy-start.4
  15.8 0.0 copy-start.5
  15.8 1.8 %copy.21 = bf16[48,16,256]{2,1,0:T(8,128)(2,1)S(1)} copy(bf16[48,16,256]{0,2,1:T(8,128)(2,1)} %bitcast.35) | data formatting | bytes 786432 | tf_op jit(solution)/shard_map/dot_general | solution.py:25
  17.6 0.0 copy-done
  17.6 1.3 %fusion.15 = (f32[48,16]{1,0:T(8,128)S(1)}, f32[48,16,256]{2,1,0:T(8,128)S(1)}) fusion(bf16[48,16,256]{2,1,0:T(8,128)(2,1)S(1)} %copy.21, bf16[256,256]{1,0:T(8,128)(2,1)S(1)} %copy-done, bf16[48,16,256]{2,1,0:T(8,128)(2,1)} %param.11), kind=kOutput, calls=%fused_computation.26 | convolution fusion | flops 101252352 | bytes 1707008 | tf_op jit(solution)/shard_map/dot_general | solution.py:25
  19.0 0.3 multiply_reduce_fusion
  19.3 0.0 copy-done.8
  19.3 0.3 multiply_convert_fusion.hid
  19.6 0.0 copy-done.1
  19.6 0.0 copy-done.2
  19.6 0.0 copy-done.3
  19.6 0.0 copy-done.4
  19.6 0.0 copy-done.5
  19.6 89.0 %shard_map.109 = bf16[48,16,256]{2,1,0:T(8,128)(2,1)S(1)} custom-call(bf16[48,16,256]{2,1,0:T(8,128)(2,1)S(1)} %multiply_convert_fusion.hid, bf16[256,256]{1,0:T(8,128)(2,1)S(1)} %copy-done.1, bf16[256,256]{1,0:T(8,128)(2,1)S(1)} %copy-done.2, bf16[256,256]{1,0:T(8,128)(2,1)S(1)} %copy-done.3, bf16[256,256]{1,0:T(8,128)(2,1)S(1)} %copy-done.4, ...), custom_call_target="tpu_custom_call" | custom-call | tf_op jit(solution)/shard_map/pallas_call | solution.py:311
  108.6 0.7 copy.27
  (4 shorter events, 0.0 us)
Async XLA Ops:
  0.0 17.6 %copy-start = (bf16[256,256]{1,0:T(8,128)(2,1)S(1)}, bf16[256,256]{1,0:T(8,128)(2,1)}, u32[]{:S(2)}) copy-start(bf16[256,256]{1,0:T(8,128)(2,1)} %param.15) | copy-start | bytes 393220
  5.6 3.5 %copy-start.6 = (bf16[48,16,256]{2,1,0:T(8,128)(2,1)S(1)}, bf16[48,16,256]{2,1,0:T(8,128)(2,1)}, u32[]{:S(2)}) copy-start(bf16[48,16,256]{2,1,0:T(8,128)(2,1)} %param.11) | copy-start | bytes 1179652
  5.6 3.5 %copy-start.7 = (bf16[256,256]{1,0:T(8,128)(2,1)S(1)}, bf16[256,256]{1,0:T(8,128)(2,1)}, u32[]{:S(2)}) copy-start(bf16[256,256]{1,0:T(8,128)(2,1)} %param.14) | copy-start | bytes 393220
  15.7 3.6 %copy-start.8 = (f32[256]{0:T(256)S(1)}, f32[256]{0:T(256)}, u32[]{:S(2)}) copy-start(f32[256]{0:T(256)} %param.20) | copy-start | bytes 3076
  15.7 3.9 %copy-start.1 = (bf16[256,256]{1,0:T(8,128)(2,1)S(1)}, bf16[256,256]{1,0:T(8,128)(2,1)}, u32[]{:S(2)}) copy-start(bf16[256,256]{1,0:T(8,128)(2,1)} %wq.1) | copy-start | bytes 393220
  15.7 3.9 %copy-start.2 = (bf16[256,256]{1,0:T(8,128)(2,1)S(1)}, bf16[256,256]{1,0:T(8,128)(2,1)}, u32[]{:S(2)}) copy-start(bf16[256,256]{1,0:T(8,128)(2,1)} %wk.1) | copy-start | bytes 393220
  15.7 3.9 %copy-start.3 = (bf16[256,256]{1,0:T(8,128)(2,1)S(1)}, bf16[256,256]{1,0:T(8,128)(2,1)}, u32[]{:S(2)}) copy-start(bf16[256,256]{1,0:T(8,128)(2,1)} %wv.1) | copy-start | bytes 393220
  15.7 3.9 %copy-start.4 = (bf16[256,256]{1,0:T(8,128)(2,1)S(1)}, bf16[256,256]{1,0:T(8,128)(2,1)}, u32[]{:S(2)}) copy-start(bf16[256,256]{1,0:T(8,128)(2,1)} %wo.1) | copy-start | bytes 393220
  15.8 3.9 %copy-start.5 = (f32[256]{0:T(256)S(1)}, f32[256]{0:T(256)}, u32[]{:S(2)}) copy-start(f32[256]{0:T(256)} %param.21) | copy-start | bytes 3076
